TPU v7x, 32 devices: a whole 2x2x4 slice. The times are simulated.
32 devices in a mesh: dp: 8 (over z, core), expert: 4 (over y, x).
Axes of the slice: x: 2, y: 2, z: 4, core: 2. Of those that a mesh axis runs over, the one named last changes fastest.
Arguments:
- tokens: bfloat16 [4, 1024, 3584], P('expert', 'dp'), may hold values from -6 to 6
- grad_out: bfloat16 [4, 1024, 3584], P('expert', 'dp'), may hold values from -6 to 6
- route_ids: int32 [4, 1024], P('expert', 'dp'), may hold values from 0 to 3, as said below
- route_gates: float32 [4, 1024], P('expert', 'dp'), may hold values from 0.2 to 1
- w_gate: bfloat16 [4, 3584, 1024], P('expert', 'dp'), may hold values from -0.09375 to 0.09375
- w_up: bfloat16 [4, 3584, 1024], P('expert', 'dp'), may hold values from -0.09375 to 0.09375
- w_down: bfloat16 [4, 1024, 3584], P('expert', 'dp'), may hold values from -0.1875 to 0.1875
Outputs:
- moe_out: bfloat16 [4, 1024, 3584], P('expert', 'dp')
- input_grad: bfloat16 [4, 1024, 3584], P('expert', None, 'dp')
- gate_grad: float32 [4, 1024], P('expert', 'dp')
Inputs may be any that keep to these rules, and one draw needn't show every extreme that they name: `route_ids`: among the 128 tokens of one device at most 80 name the same expert; one expert is named by exactly 80 tokens of every device; on one device the counts of the other experts differ by at most one.
All inputs are finite; a program needn't handle non-finite values.
Results may differ from a plain program's by a relative error of at most 0.0057.
Values may be sent and summed in bfloat16 or wider, within the bound.
A program may use at most 128 MiB of HBM per device.

v0:
```python
import jax
import jax.numpy as jnp
from jax import lax
from jax.sharding import PartitionSpec as P


def slot_table(route_line, expert_count, capacity):
    chosen = (route_line[:, None] == jnp.arange(expert_count, dtype=jnp.int32)[None, :]).astype(
        jnp.int32
    )
    placed = jnp.sum((jnp.cumsum(chosen, axis=0) - 1) * chosen, axis=1)
    return route_line * capacity + placed


def local(tokens, grad_out, route_ids, route_gates, w_gate, w_up, w_down):
    expert_count = lax.axis_size("expert")
    tok_count = tokens.shape[1]
    width = tokens.shape[2]
    capacity = max(2, 5 * tok_count // (2 * expert_count))
    own_ids = route_ids[0]
    own_slots = slot_table(own_ids, expert_count, capacity)
    slot_owner = jnp.full((expert_count * capacity,), tok_count, jnp.int32)
    slot_owner = slot_owner.at[own_slots].set(jnp.arange(tok_count, dtype=jnp.int32))
    own_tokens = tokens[0]
    own_grad = grad_out[0]
    gate_column = route_gates[0][:, None]
    scaled_grad = (gate_column * own_grad.astype(jnp.float32)).astype(jnp.bfloat16)
    zero_row = jnp.zeros((1, width), jnp.bfloat16)
    send_tokens = jnp.concatenate([own_tokens, zero_row])[slot_owner].reshape(
        expert_count, capacity, width
    )
    send_grad = jnp.concatenate([scaled_grad, zero_row])[slot_owner].reshape(
        expert_count, capacity, width
    )
    arrived_tokens = lax.all_to_all(send_tokens, "expert", split_axis=0, concat_axis=0, tiled=True)
    routed = arrived_tokens.reshape(expert_count * capacity, width)
    full_gate, full_up, full_down = (
        lax.all_gather(w_gate, "dp", axis=1, tiled=True),
        lax.all_gather(w_up, "dp", axis=1, tiled=True),
        lax.all_gather(w_down, "dp", axis=1, tiled=True),
    )
    gate_matrix = full_gate[0]
    up_matrix = full_up[0]
    down_matrix = full_down[0]
    gate_pre = jnp.dot(routed, gate_matrix, preferred_element_type=jnp.float32)
    up_pre = jnp.dot(routed, up_matrix, preferred_element_type=jnp.float32)
    sigmoid_gate = jax.nn.sigmoid(gate_pre)
    silu_gate = gate_pre * sigmoid_gate
    hidden = (silu_gate * up_pre).astype(jnp.bfloat16)
    expert_out = jnp.dot(hidden, down_matrix, preferred_element_type=jnp.float32).astype(
        jnp.bfloat16
    )
    returned = lax.all_to_all(
        expert_out.reshape(expert_count, capacity, width),
        "expert",
        split_axis=0,
        concat_axis=0,
        tiled=True,
    )
    token_out = returned.reshape(expert_count * capacity, width)[own_slots]
    moe_out = (gate_column * token_out.astype(jnp.float32)).astype(jnp.bfloat16)
    gate_grad = jnp.sum(own_grad.astype(jnp.float32) * token_out.astype(jnp.float32), axis=1)
    arrived_grad = lax.all_to_all(send_grad, "expert", split_axis=0, concat_axis=0, tiled=True)
    routed_grad = arrived_grad.reshape(expert_count * capacity, width)
    hidden_grad = jnp.dot(routed_grad, down_matrix.T, preferred_element_type=jnp.float32)
    gate_pre_grad = (
        hidden_grad * up_pre * sigmoid_gate * (1.0 + gate_pre * (1.0 - sigmoid_gate))
    ).astype(jnp.bfloat16)
    up_pre_grad = (hidden_grad * silu_gate).astype(jnp.bfloat16)
    total = jnp.dot(gate_pre_grad, gate_matrix.T, preferred_element_type=jnp.float32)
    input_rows = (
        total + jnp.dot(up_pre_grad, up_matrix.T, preferred_element_type=jnp.float32)
    ).astype(jnp.bfloat16)
    home_rows = lax.all_to_all(
        input_rows.reshape(expert_count, capacity, width),
        "expert",
        split_axis=0,
        concat_axis=0,
        tiled=True,
    )
    token_grad = home_rows.reshape(expert_count * capacity, width)[own_slots]
    input_grad = lax.all_to_all(token_grad[None], "dp", split_axis=2, concat_axis=1, tiled=True)
    return (moe_out[None], input_grad, gate_grad[None])


def solution(mesh):
    in_specs = (
        P("expert", "dp", None),
        P("expert", "dp", None),
        P("expert", "dp"),
        P("expert", "dp"),
        P("expert", "dp", None),
        P("expert", "dp", None),
        P("expert", "dp", None),
    )
    out_specs = (P("expert", "dp", None), P("expert", None, "dp"), P("expert", "dp"))
    return jax.shard_map(local, mesh=mesh, in_specs=in_specs, out_specs=out_specs, check_vma=False)
```

profile of v0, /device:TPU:0, one launch (start us, length us, event | category | flops | bytes accessed | tf_op | source)
XLA Modules:
  0.0 416.3 jit_solution(1568874448295475949)
XLA Ops:
  11.0 3.1 gather_fusion
  14.1 32.7 %all_to_all.38 = bf16[4,80,3584]{2,1,0:T(8,128)(2,1)} all-to-all(bf16[4,80,3584]{2,1,0:T(8,128)(2,1)S(1)} %bitcast.67), channel_id=1, replica_groups=mesh['dp'=8,'expert'=4] {'expert'}, dimensions={0} | all-to-all | bytes 4587520 | tf_op jit(solution)/shard_map/all_to_all | solution.py:35
  46.8 39.0 %all-gather.4.cloned.1.call-done = bf16[1,3584,1024]{2,1,0:T(8,128)(2,1)} async-done(((bf16[1,448,1024]{2,1,0:T(8,128)(2,1)}), bf16[1,3584,1024]{2,1,0:T(8,128)(2,1)}) %all-gather.4.cloned.1.call-update) | async-done | bytes 7340048 | tf_op jit(solution)/shard_map/all_gather | solution.py:38
  85.8 7.5 %fusion.10 = f32[320,1024]{1,0:T(8,128)} fusion(bf16[320,3584]{1,0:T(8,128)(2,1)} %bitcast.72, bf16[1,3584,1024]{2,1,0:T(8,128)(2,1)} %all-gather.4.cloned.1.call-done), kind=kOutput, calls=%fused_computation.15 | convolution fusion | flops 2348810240 | bytes 10944512 | tf_op jit(solution)/shard_map/dot_general | solution.py:45
  93.3 66.2 %all-gather.6.cloned.1.call-done = bf16[1,3584,1024]{2,1,0:T(8,128)(2,1)} async-done(((bf16[1,448,1024]{2,1,0:T(8,128)(2,1)}), bf16[1,3584,1024]{2,1,0:T(8,128)(2,1)}) %all-gather.6.cloned.1.call-update) | async-done | bytes 7340048 | tf_op jit(solution)/shard_map/all_gather | solution.py:39
  159.5 6.8 %fusion.6 = f32[320,1024]{1,0:T(8,128)} fusion(bf16[320,3584]{1,0:T(8,128)(2,1)S(1)} %bitcast.73, bf16[1,3584,1024]{2,1,0:T(8,128)(2,1)} %all-gather.6.cloned.1.call-done), kind=kOutput, calls=%fused_computation.11 | convolution fusion | flops 2348810240 | bytes 10944512 | tf_op jit(solution)/shard_map/dot_general | solution.py:46
  166.2 66.9 %all-gather.8.cloned.1.call-done = bf16[1,1024,3584]{2,1,0:T(8,128)(2,1)} async-done(((bf16[1,128,3584]{2,1,0:T(8,128)(2,1)}), bf16[1,1024,3584]{2,1,0:T(8,128)(2,1)}) %all-gather.8.cloned.1.call-update) | async-done | bytes 7340048 | tf_op jit(solution)/shard_map/all_gather | solution.py:40
  233.1 7.9 %fusion.18 = bf16[320,3584]{1,0:T(8,128)(2,1)} fusion(bf16[1,1024,3584]{2,1,0:T(8,128)(2,1)} %all-gather.8.cloned.1.call-done, f32[320,1024]{1,0:T(8,128)} %fusion.6, f32[320,1024]{1,0:T(8,128)} %fusion.10), kind=kOutput, calls=%fused_computation.19 | convolution fusion | flops 2351923200 | bytes 12255232 | tf_op jit(solution)/shard_map/dot_general | solution.py:50
  241.0 3.7 all-to-all-start.1
  244.7 27.6 %all-to-all-done.1 = bf16[4,80,3584]{2,1,0:T(8,128)(2,1)S(1)} async-done(((bf16[4,80,3584]{2,1,0:T(8,128)(2,1)}), bf16[4,80,3584]{2,1,0:T(8,128)(2,1)S(1)}, u32[]{:S(2)}, u32[]{:S(2)}) %all-to-all-start.1) | async-done | bytes 2293792 | tf_op jit(solution)/shard_map/all_to_all | solution.py:53
  273.4 2.5 fusion.24
  276.0 3.1 gather_fusion.2
  279.1 30.1 %all_to_all.39 = bf16[4,80,3584]{2,1,0:T(8,128)(2,1)S(1)} all-to-all(bf16[4,80,3584]{2,1,0:T(8,128)(2,1)S(1)} %bitcast.66), channel_id=1, replica_groups=mesh['dp'=8,'expert'=4] {'expert'}, dimensions={0} | all-to-all | bytes 4587520 | tf_op jit(solution)/shard_map/all_to_all | solution.py:63
  309.3 5.8 %fusion = f32[320,1024]{1,0:T(8,128)S(1)} fusion(bf16[320,3584]{1,0:T(8,128)(2,1)S(1)} %bitcast.76, bf16[1,1024,3584]{2,1,0:T(8,128)(2,1)} %all-gather.8.cloned.1.call-done), kind=kOutput, calls=%fused_computation.5 | convolution fusion | flops 2348810240 | bytes 10944512 | tf_op jit(solution)/shard_map/dot_general | solution.py:65
  316.2 4.8 %fusion.4 = f32[320,3584]{1,0:T(8,128)} fusion(bf16[1,3584,1024]{2,1,0:T(8,128)(2,1)S(1)} %bitcast.87, f32[320,1024]{1,0:T(8,128)S(1)} %fusion, f32[320,1024]{1,0:T(8,128)S(1)} %copy-done.6), kind=kOutput, calls=%fused_computation.9 | convolution fusion | flops 2350776320 | bytes 14548992 | tf_op jit(solution)/shard_map/dot_general | solution.py:72
  320.9 6.0 %fusion.15 = bf16[320,3584]{1,0:T(8,128)(2,1)S(1)} fusion(f32[320,3584]{1,0:T(8,128)} %fusion.4, bf16[1,3584,1024]{2,1,0:T(8,128)(2,1)S(1)} %bitcast.85, f32[320,1024]{1,0:T(8,128)S(1)} %copy-done.6, f32[320,1024]{1,0:T(8,128)} %copy-done.7, f32[320,1024]{1,0:T(8,128)} %fusion.6), kind=kOutput, calls=%fused_computation.18 | convolution fusion | flops 2354380800 | bytes 18153472 | tf_op jit(solution)/shard_map/dot_general | solution.py:70
  326.9 28.4 %all_to_all.40 = bf16[4,80,3584]{2,1,0:T(8,128)(2,1)S(1)} all-to-all(bf16[4,80,3584]{2,1,0:T(8,128)(2,1)S(1)} %bitcast.75), channel_id=1, replica_groups=mesh['dp'=8,'expert'=4] {'expert'}, dimensions={0} | all-to-all | bytes 4587520 | tf_op jit(solution)/shard_map/all_to_all | solution.py:74
  356.5 2.5 copy.14
  359.5 19.7 %reduce = bf16[3584,128]{1,0:T(8,128)(2,1)S(1)} reduce(bf16[3584,1,128]{2,1,0:T(2,128)(2,1)S(1)} %bitcast.68, bf16[]{:T(256)} %broadcast.103), dimensions={1}, to_apply=%bitcast.58.reduce_sub_computation | reduce | bytes 1835010
  379.2 1.1 reshape.155
  380.3 3.6 all-to-all-start.4
  383.9 1.1 fusion.22
  385.0 22.6 %all-to-all-done.4 = bf16[8,2,28672]{2,1,0:T(2,128)(2,1)S(1)} async-done(((bf16[8,2,28672]{2,1,0:T(2,128)(2,1)}), bf16[8,2,28672]{2,1,0:T(2,128)(2,1)S(1)}, u32[]{:S(2)}, u32[]{:S(2)}) %all-to-all-start.4) | async-done | bytes 917536 | tf_op jit(solution)/shard_map/all_to_all | solution.py:82
  408.6 1.2 copy.19
  (48 shorter events, 8.6 us)
Async XLA Ops:
  7.2 2.2 copy-start.4
  7.2 2.5 copy-start.3
  7.2 78.6 %all-gather.4.cloned.1.call-start = ((), (), s32[]{:S(2)}) async-start(), calls=%async_computation.5 | async-start | bytes 8257536 | tf_op jit(solution)/shard_map/all_gather | solution.py:38
  7.9 151.5 %all-gather.6.cloned.1.call-start = ((), (), s32[]{:S(2)}) async-start(), calls=%async_computation.6 | async-start | bytes 8257536 | tf_op jit(solution)/shard_map/all_gather | solution.py:39
  8.7 224.5 %all-gather.8.cloned.1.call-start = ((), (), s32[]{:S(2)}) async-start(), calls=%async_computation.7 | async-start | bytes 8257536 | tf_op jit(solution)/shard_map/all_gather | solution.py:40
  85.8 73.7 %copy-start.2 = (bf16[4,80,3584]{2,1,0:T(8,128)(2,1)S(1)}, bf16[4,80,3584]{2,1,0:T(8,128)(2,1)}, u32[]{:S(2)}) copy-start(bf16[4,80,3584]{2,1,0:T(8,128)(2,1)} %all_to_all.38) | copy-start | bytes 6881284
  241.0 31.3 %all-to-all-start.1 = ((bf16[4,80,3584]{2,1,0:T(8,128)(2,1)}), bf16[4,80,3584]{2,1,0:T(8,128)(2,1)S(1)}, u32[]{:S(2)}, u32[]{:S(2)}) async-start(bf16[4,80,3584]{2,1,0:T(8,128)(2,1)} %bitcast.74), calls=%async_computation.1 | async-start | bytes 4587520 | tf_op jit(solution)/shard_map/all_to_all | solution.py:53
  272.3 1.1 copy-start.5
  273.4 2.5 copy-start
  279.1 37.1 %slice-start.2 = ((s8[7340032]{0:T(1024)(128)(4,1)}), s8[4194304]{0:T(1024)(128)(4,1)S(1)}, s32[]{:S(2)}) async-start(s8[7340032]{0:T(1024)(128)(4,1)} %bitcast.86), calls=%async_computation.10 | async-start | bytes 8388608
  309.3 6.9 %slice-start.3 = ((s8[7340032]{0:T(1024)(128)(4,1)}), s8[3145728]{0:T(1024)(128)(4,1)S(1)}, s32[]{:S(2)}) async-start(s8[7340032]{0:T(1024)(128)(4,1)} %bitcast.86), calls=%async_computation.11 | async-start | bytes 6291456
  309.3 6.9 %copy-start.6 = (f32[320,1024]{1,0:T(8,128)S(1)}, f32[320,1024]{1,0:T(8,128)}, u32[]{:S(2)}) copy-start(f32[320,1024]{1,0:T(8,128)} %fusion.10) | copy-start | bytes 3932164
  309.3 11.7 %slice-start = ((s8[7340032]{0:T(1024)(128)(4,1)}), s8[4194304]{0:T(1024)(128)(4,1)S(1)}, s32[]{:S(2)}) async-start(s8[7340032]{0:T(1024)(128)(4,1)} %bitcast.84), calls=%async_computation.8 | async-start | bytes 8388608
  315.1 1.1 copy-start.7
  316.2 4.8 %slice-start.1 = ((s8[7340032]{0:T(1024)(128)(4,1)}), s8[3145728]{0:T(1024)(128)(4,1)S(1)}, s32[]{:S(2)}) async-start(s8[7340032]{0:T(1024)(128)(4,1)} %bitcast.84), calls=%async_computation.9 | async-start | bytes 6291456
  379.2 4.7 %copy-start.1 = (bf16[128,3584]{1,0:T(8,128)(2,1)S(1)}, bf16[128,3584]{1,0:T(8,128)(2,1)}, u32[]{:S(2)}) copy-start(bf16[128,3584]{1,0:T(8,128)(2,1)} %copy-done) | copy-start | bytes 2752516
  380.3 27.3 %all-to-all-start.4 = ((bf16[8,2,28672]{2,1,0:T(2,128)(2,1)}), bf16[8,2,28672]{2,1,0:T(2,128)(2,1)S(1)}, u32[]{:S(2)}, u32[]{:S(2)}) async-start(bf16[8,2,28672]{2,1,0:T(2,128)(2,1)} %reshape.155), calls=%async_computation.4 | async-start | bytes 1835008 | tf_op jit(solution)/shard_map/all_to_all | solution.py:82
Sparse Core Ops, SparseCore 0:
  9.7 76.0 all-gather.3
  87.4 71.9 all-gather.5
  161.1 71.9 all-gather.7
where the time goes:
time: 417 us; the launch traced here: 416 us
  waiting for transfers between devices  224 us (54%)
  blocking collectives  91.3 us (22%)
  matrix products  38.7 us (9%)
  other arithmetic  23.7 us (6%)
  local copies, waits for them, and re-layouts  17.1 us (4%)
  between operations  14 us (3%)
  starting transfers between devices  7.35 us (2%)
    all_gather x1, waiting for transfers between devices, local(): lax.all_gather(w_down, 'dp', axis=1, tiled=True)  66.9 us
    all_gather x1, waiting for transfers between devices, local(): lax.all_gather(w_up, 'dp', axis=1, tiled=True)  66.2 us
    all_gather x1, waiting for transfers between devices, local(): lax.all_gather(w_gate, 'dp', axis=1, tiled=True)  39 us
    all_to_all x1, blocking collectives, local(): lax.all_to_all(send_tokens, 'expert', split_axis=0, concat_axis=0, tiled=...  32.7 us
    all_to_all x1, blocking collectives, local(): lax.all_to_all(send_grad, 'expert', split_axis=0, concat_axis=0, tiled=True)  30.1 us
    all_to_all x1, blocking collectives, local(): lax.all_to_all(input_rows.reshape(expert_count, capacity, width), 'expert...  28.4 us
    all_to_all x1, waiting for transfers between devices, local(): lax.all_to_all(expert_out.reshape(expert_count, capacity, width), 'expert...  27.6 us
    all_to_all x1, waiting for transfers between devices, local(): lax.all_to_all(token_grad[None], 'dp', split_axis=2, concat_axis=1, tiled...  22.6 us
  transfers between devices with their start and end apart: 5, of which 5 were waited for; matrix products, arithmetic and copies ran while one was open for 5% of the time, Pallas kernels for 0%

commit v1 on v0

--- a/solution.py
+++ b/solution.py
@@ -79,7 +79,12 @@
         tiled=True,
     )
     token_grad = home_rows.reshape(expert_count * capacity, width)[own_slots]
-    input_grad = lax.all_to_all(token_grad[None], "dp", split_axis=2, concat_axis=1, tiled=True)
+    input_grad = jnp.concatenate(
+        lax.all_to_all(
+            jnp.stack(jnp.split(token_grad[None], lax.axis_size("dp"), axis=2)), "dp", 0, 0
+        ),
+        axis=1,
+    )
     return (moe_out[None], input_grad, gate_grad[None])
 
 

time: 417 us -> 393 us (0.942)
  other arithmetic: 23.7 us -> 4.06 us
    unnamed x3 -> x2, other arithmetic: 19.7 us -> 0.01 us
where the time goes in v1:
time: 393 us
  waiting for transfers between devices  224 us (57%)
  blocking collectives  91.3 us (23%)
  matrix products  38.6 us (10%)
  between operations  14 us (4%)
  local copies, waits for them, and re-layouts  13.5 us (3%)
  starting transfers between devices  7.35 us (2%)
  other arithmetic  4.06 us (1%)
    all_gather x1, waiting for transfers between devices, local(): lax.all_gather(w_down, 'dp', axis=1, tiled=True)  66.9 us
    all_gather x1, waiting for transfers between devices, local(): lax.all_gather(w_up, 'dp', axis=1, tiled=True)  66.2 us
    all_gather x1, waiting for transfers between devices, local(): lax.all_gather(w_gate, 'dp', axis=1, tiled=True)  39 us
    all_to_all x1, blocking collectives, local(): lax.all_to_all(send_tokens, 'expert', split_axis=0, concat_axis=0, tiled=...  32.7 us
    all_to_all x1, blocking collectives, local(): lax.all_to_all(send_grad, 'expert', split_axis=0, concat_axis=0, tiled=True)  30.1 us
    all_to_all x1, blocking collectives, local(): lax.all_to_all(input_rows.reshape(expert_count, capacity, width), 'expert...  28.4 us
    all_to_all x1, waiting for transfers between devices, local(): lax.all_to_all(expert_out.reshape(expert_count, capacity, width), 'expert...  27.6 us
    all_to_all x1, waiting for transfers between devices, local(): lax.all_to_all(jnp.stack(jnp.split(token_grad[None], lax.axis_size('dp'),...  22.6 us
  transfers between devices with their start and end apart: 5, of which 5 were waited for; matrix products, arithmetic and copies ran while one was open for 5% of the time, Pallas kernels for 0%

profile of v1, /device:TPU:0, one launch (start us, length us, event | category | flops | bytes accessed | tf_op | source)
XLA Modules:
  0.0 393.1 jit_solution(5612317303807939787)
XLA Ops:
  11.0 3.1 gather_fusion
  14.1 32.7 %all_to_all.25 = bf16[4,80,3584]{2,1,0:T(8,128)(2,1)} all-to-all(bf16[4,80,3584]{2,1,0:T(8,128)(2,1)S(1)} %bitcast.96), channel_id=1, replica_groups=mesh['dp'=8,'expert'=4] {'expert'}, dimensions={0} | all-to-all | bytes 4587520 | tf_op jit(solution)/shard_map/all_to_all | solution.py:35
  46.8 39.0 %all-gather.4.cloned.1.call-done = bf16[1,3584,1024]{2,1,0:T(8,128)(2,1)} async-done(((bf16[1,448,1024]{2,1,0:T(8,128)(2,1)}), bf16[1,3584,1024]{2,1,0:T(8,128)(2,1)}) %all-gather.4.cloned.1.call-update) | async-done | bytes 7340048 | tf_op jit(solution)/shard_map/all_gather | solution.py:38
  85.8 7.5 %fusion.10 = f32[320,1024]{1,0:T(8,128)} fusion(bf16[320,3584]{1,0:T(8,128)(2,1)} %bitcast.105, bf16[1,3584,1024]{2,1,0:T(8,128)(2,1)} %all-gather.4.cloned.1.call-done), kind=kOutput, calls=%fused_computation.15 | convolution fusion | flops 2348810240 | bytes 10944512 | tf_op jit(solution)/shard_map/dot_general | solution.py:45
  93.3 66.2 %all-gather.6.cloned.1.call-done = bf16[1,3584,1024]{2,1,0:T(8,128)(2,1)} async-done(((bf16[1,448,1024]{2,1,0:T(8,128)(2,1)}), bf16[1,3584,1024]{2,1,0:T(8,128)(2,1)}) %all-gather.6.cloned.1.call-update) | async-done | bytes 7340048 | tf_op jit(solution)/shard_map/all_gather | solution.py:39
  159.5 6.8 %fusion.6 = f32[320,1024]{1,0:T(8,128)} fusion(bf16[320,3584]{1,0:T(8,128)(2,1)S(1)} %bitcast.106, bf16[1,3584,1024]{2,1,0:T(8,128)(2,1)} %all-gather.6.cloned.1.call-done), kind=kOutput, calls=%fused_computation.11 | convolution fusion | flops 2348810240 | bytes 10944512 | tf_op jit(solution)/shard_map/dot_general | solution.py:46
  166.2 66.9 %all-gather.8.cloned.1.call-done = bf16[1,1024,3584]{2,1,0:T(8,128)(2,1)} async-done(((bf16[1,128,3584]{2,1,0:T(8,128)(2,1)}), bf16[1,1024,3584]{2,1,0:T(8,128)(2,1)}) %all-gather.8.cloned.1.call-update) | async-done | bytes 7340048 | tf_op jit(solution)/shard_map/all_gather | solution.py:40
  233.1 7.8 %fusion.18 = bf16[320,3584]{1,0:T(8,128)(2,1)} fusion(bf16[1,1024,3584]{2,1,0:T(8,128)(2,1)} %all-gather.8.cloned.1.call-done, f32[320,1024]{1,0:T(8,128)} %fusion.6, f32[320,1024]{1,0:T(8,128)} %fusion.10), kind=kOutput, calls=%fused_computation.19 | convolution fusion | flops 2351923200 | bytes 12255232 | tf_op jit(solution)/shard_map/dot_general | solution.py:50
  241.0 3.7 all-to-all-start.1
  244.7 27.6 %all-to-all-done.1 = bf16[4,80,3584]{2,1,0:T(8,128)(2,1)S(1)} async-done(((bf16[4,80,3584]{2,1,0:T(8,128)(2,1)}), bf16[4,80,3584]{2,1,0:T(8,128)(2,1)S(1)}, u32[]{:S(2)}, u32[]{:S(2)}) %all-to-all-start.1) | async-done | bytes 2293792 | tf_op jit(solution)/shard_map/all_to_all | solution.py:53
  272.3 1.1 gather_fusion.1
  273.4 2.5 fusion.24
  275.9 3.1 gather_fusion.2
  279.1 30.1 %all_to_all.26 = bf16[4,80,3584]{2,1,0:T(8,128)(2,1)S(1)} all-to-all(bf16[4,80,3584]{2,1,0:T(8,128)(2,1)S(1)} %bitcast.95), channel_id=1, replica_groups=mesh['dp'=8,'expert'=4] {'expert'}, dimensions={0} | all-to-all | bytes 4587520 | tf_op jit(solution)/shard_map/all_to_all | solution.py:63
  309.2 5.8 %fusion = f32[320,1024]{1,0:T(8,128)S(1)} fusion(bf16[320,3584]{1,0:T(8,128)(2,1)S(1)} %bitcast.109, bf16[1,1024,3584]{2,1,0:T(8,128)(2,1)} %all-gather.8.cloned.1.call-done), kind=kOutput, calls=%fused_computation.5 | convolution fusion | flops 2348810240 | bytes 10944512 | tf_op jit(solution)/shard_map/dot_general | solution.py:65
  315.0 1.1 copy-done.7
  316.1 4.8 %fusion.4 = f32[320,3584]{1,0:T(8,128)} fusion(bf16[1,3584,1024]{2,1,0:T(8,128)(2,1)S(1)} %bitcast.119, f32[320,1024]{1,0:T(8,128)S(1)} %fusion, f32[320,1024]{1,0:T(8,128)S(1)} %copy-done.6), kind=kOutput, calls=%fused_computation.9 | convolution fusion | flops 2350776320 | bytes 14548992 | tf_op jit(solution)/shard_map/dot_general | solution.py:72
  320.9 6.0 %fusion.15 = bf16[320,3584]{1,0:T(8,128)(2,1)S(1)} fusion(f32[320,3584]{1,0:T(8,128)} %fusion.4, bf16[1,3584,1024]{2,1,0:T(8,128)(2,1)S(1)} %bitcast.117, f32[320,1024]{1,0:T(8,128)S(1)} %copy-done.6, f32[320,1024]{1,0:T(8,128)} %copy-done.7, f32[320,1024]{1,0:T(8,128)} %fusion.6), kind=kOutput, calls=%fused_computation.18 | convolution fusion | flops 2354380800 | bytes 18153472 | tf_op jit(solution)/shard_map/dot_general | solution.py:70
  326.9 28.4 %all_to_all.27 = bf16[4,80,3584]{2,1,0:T(8,128)(2,1)S(1)} all-to-all(bf16[4,80,3584]{2,1,0:T(8,128)(2,1)S(1)} %bitcast.108), channel_id=1, replica_groups=mesh['dp'=8,'expert'=4] {'expert'}, dimensions={0} | all-to-all | bytes 4587520 | tf_op jit(solution)/shard_map/all_to_all | solution.py:74
  355.3 1.1 gather_fusion.3
  356.9 1.3 copy.12
  358.2 3.6 all-to-all-start.4
  361.8 1.1 fusion.22
  362.9 22.6 %all-to-all-done.4 = bf16[8,1,128,448]{2,3,1,0:T(8,128)(2,1)S(1)} async-done(((bf16[8,1,128,448]{2,3,1,0:T(8,128)(2,1)}), bf16[8,1,128,448]{2,3,1,0:T(8,128)(2,1)S(1)}, u32[]{:S(2)}, u32[]{:S(2)}) %all-to-all-start.4) | async-done | bytes 917536 | tf_op jit(solution)/shard_map/all_to_all | solution.py:83
  (51 shorter events, 5.3 us)
Async XLA Ops:
  7.2 2.2 copy-start.4
  7.2 2.5 copy-start.3
  7.2 78.6 %all-gather.4.cloned.1.call-start = ((), (), s32[]{:S(2)}) async-start(), calls=%async_computation.5 | async-start | bytes 8257536 | tf_op jit(solution)/shard_map/all_gather | solution.py:38
  7.9 151.5 %all-gather.6.cloned.1.call-start = ((), (), s32[]{:S(2)}) async-start(), calls=%async_computation.6 | async-start | bytes 8257536 | tf_op jit(solution)/shard_map/all_gather | solution.py:39
  8.7 224.5 %all-gather.8.cloned.1.call-start = ((), (), s32[]{:S(2)}) async-start(), calls=%async_computation.7 | async-start | bytes 8257536 | tf_op jit(solution)/shard_map/all_gather | solution.py:40
  85.8 73.7 %copy-start.2 = (bf16[4,80,3584]{2,1,0:T(8,128)(2,1)S(1)}, bf16[4,80,3584]{2,1,0:T(8,128)(2,1)}, u32[]{:S(2)}) copy-start(bf16[4,80,3584]{2,1,0:T(8,128)(2,1)} %all_to_all.25) | copy-start | bytes 6881284
  241.0 31.3 %all-to-all-start.1 = ((bf16[4,80,3584]{2,1,0:T(8,128)(2,1)}), bf16[4,80,3584]{2,1,0:T(8,128)(2,1)S(1)}, u32[]{:S(2)}, u32[]{:S(2)}) async-start(bf16[4,80,3584]{2,1,0:T(8,128)(2,1)} %bitcast.107), calls=%async_computation.1 | async-start | bytes 4587520 | tf_op jit(solution)/shard_map/all_to_all | solution.py:53
  272.3 1.1 copy-start.5
  273.4 2.5 copy-start
  279.1 37.0 %slice-start.2 = ((s8[7340032]{0:T(1024)(128)(4,1)}), s8[4194304]{0:T(1024)(128)(4,1)S(1)}, s32[]{:S(2)}) async-start(s8[7340032]{0:T(1024)(128)(4,1)} %bitcast.118), calls=%async_computation.10 | async-start | bytes 8388608
  309.2 6.9 %slice-start.3 = ((s8[7340032]{0:T(1024)(128)(4,1)}), s8[3145728]{0:T(1024)(128)(4,1)S(1)}, s32[]{:S(2)}) async-start(s8[7340032]{0:T(1024)(128)(4,1)} %bitcast.118), calls=%async_computation.11 | async-start | bytes 6291456
  309.2 6.9 %copy-start.6 = (f32[320,1024]{1,0:T(8,128)S(1)}, f32[320,1024]{1,0:T(8,128)}, u32[]{:S(2)}) copy-start(f32[320,1024]{1,0:T(8,128)} %fusion.10) | copy-start | bytes 3932164
  309.2 11.7 %slice-start = ((s8[7340032]{0:T(1024)(128)(4,1)}), s8[4194304]{0:T(1024)(128)(4,1)S(1)}, s32[]{:S(2)}) async-start(s8[7340032]{0:T(1024)(128)(4,1)} %bitcast.116), calls=%async_computation.8 | async-start | bytes 8388608
  315.0 1.1 copy-start.7
  316.1 4.8 %slice-start.1 = ((s8[7340032]{0:T(1024)(128)(4,1)}), s8[3145728]{0:T(1024)(128)(4,1)S(1)}, s32[]{:S(2)}) async-start(s8[7340032]{0:T(1024)(128)(4,1)} %bitcast.116), calls=%async_computation.9 | async-start | bytes 6291456
  356.7 5.1 %copy-start.1 = (bf16[128,3584]{1,0:T(8,128)(2,1)S(1)}, bf16[128,3584]{1,0:T(8,128)(2,1)}, u32[]{:S(2)}) copy-start(bf16[128,3584]{1,0:T(8,128)(2,1)} %copy-done) | copy-start | bytes 2752516
  358.2 27.3 %all-to-all-start.4 = ((bf16[8,1,128,448]{2,3,1,0:T(8,128)(2,1)}), bf16[8,1,128,448]{2,3,1,0:T(8,128)(2,1)S(1)}, u32[]{:S(2)}, u32[]{:S(2)}) async-start(bf16[8,1,128,448]{2,3,1,0:T(8,128)(2,1)} %copy.12), calls=%async_computation.4 | async-start | bytes 1835008 | tf_op jit(solution)/shard_map/all_to_all | solution.py:83
Sparse Core Ops, SparseCore 0:
  9.7 76.0 all-gather.3
  87.4 71.9 all-gather.5
  161.1 71.9 all-gather.7
